TPU v7x, 256 devices: a whole 4x4x8 slice. The times are simulated.
256 devices in a mesh: section: 16 (over x_hi, z), dp: 16 (over x_lo, y, core).
Axes of the slice: x: 4 (x_hi: 2, x_lo: 2; x = x_hi * 2 + x_lo), y: 4, z: 8, core: 2. Of those that a mesh axis runs over, the one named last changes fastest.
Arguments:
- grad_in: bfloat16 [16, 128, 8192], P('section', 'dp'), may hold values from -6 to 6
- weights: bfloat16 [16, 8192, 8192], P('section', 'dp'), may hold values from -0.0625 to 0.0625
- band_index: int32 [16, 8, 2], P('section'), may hold values from 0 to 15
- owner: int32 [16], replicated, may hold values from 0 to 15, each once
Outputs:
- factors: float32 [16, 16, 512, 512], P('section', 'dp')
- grad_out: bfloat16 [16, 128, 8192], P('section', 'dp')
Inputs may be any that keep to these rules, and one draw needn't show every extreme that they name: `owner`: each slot number appears exactly once.
All inputs are finite; a program needn't handle non-finite values.
Results may differ from a plain program's by a relative error of at most 0.0051.
Values may be sent and summed in bfloat16 or wider, within the bound.
A program may use at most 128 MiB of HBM per device.

v0:
```python
import jax
import jax.numpy as jnp
from jax import lax
from jax.sharding import PartitionSpec as P

D = 8192
BLK = 512
NB = 8
STEPS = 2


def passed_along(value, axis, steps):
    count = lax.axis_size(axis)
    pairs = [(source, (source + steps) % count) for source in range(count)]
    return lax.ppermute(value, axis, pairs)


def gram_blocks(old, new, pairs):
    rows = old.shape[0]
    old_b = old.reshape(rows, D // BLK, BLK)
    new_b = new.reshape(rows, D // BLK, BLK)
    left = jnp.take(old_b, pairs[:, 0], axis=1)
    right_old = jnp.take(old_b, pairs[:, 1], axis=1)
    right_new = jnp.take(new_b, pairs[:, 1], axis=1)
    own = jnp.einsum("tkb,tkc->kbc", left, right_old, preferred_element_type=jnp.float32)
    cross = jnp.einsum("tkb,tkc->kbc", left, right_new, preferred_element_type=jnp.float32)
    return jnp.concatenate([own, cross], axis=0)


def shards(grad_in, weights, band_index, owner):
    held = grad_in[0]
    w_rows = weights[0]
    pairs = band_index[0]
    tok_dev = held.shape[0]
    dp_count = lax.axis_size("dp")
    all_tokens = tok_dev * dp_count
    totals = jnp.zeros((2 * NB, BLK, BLK), jnp.float32)
    for step in range(STEPS):
        banded = lax.all_to_all(held, "dp", split_axis=1, concat_axis=0, tiled=True)
        summed = lax.psum_scatter(
            jnp.dot(banded, w_rows, preferred_element_type=jnp.float32),
            "dp",
            scatter_dimension=0,
            tiled=True,
        )
        fresh = (held.astype(jnp.float32) + summed).astype(jnp.bfloat16)
        totals = totals + gram_blocks(held, fresh, pairs)
        held = passed_along(fresh, "section", -1)
    ordered = jnp.take(totals, owner, axis=0) / float(all_tokens * STEPS)
    owned = lax.psum_scatter(ordered, "dp", scatter_dimension=0, tiled=True)
    return (owned[None], held[None])


def solution(mesh):
    return jax.shard_map(
        shards,
        mesh=mesh,
        in_specs=(
            P("section", "dp", None),
            P("section", "dp", None),
            P("section", None, None),
            P(),
        ),
        out_specs=(P("section", "dp", None, None), P("section", "dp", None)),
        check_vma=False,
    )
```

profile of v0, /device:TPU:1, one launch (start us, length us, event | category | flops | bytes accessed | tf_op | source)
XLA Modules:
  0.0 337.5 jit_solution(7443287970270801856)
XLA Ops:
  7.2 0.0 reduce-scatter.4.cloned.1.call-start
  7.2 13.1 %all_to_all.32 = bf16[8,16,512]{2,0,1:T(8,128)(2,1)S(1)} all-to-all(bf16[8,16,512]{2,0,1:T(8,128)(2,1)} %bitcast.53), channel_id=1, replica_groups=mesh['section'=16,'dp'=16] {'dp'}, dimensions={1} | all-to-all | bytes 262144 | tf_op jit(solution)/shard_map/all_to_all | solution.py:39
  20.3 0.0 copy-start.1
  20.3 6.7 %fusion.2 = f32[128,8192]{1,0:T(8,128)} fusion(bf16[1,512,8192]{2,1,0:T(8,128)(2,1)} %param.7, bf16[8,16,512]{2,0,1:T(8,128)(2,1)S(1)} %all_to_all.32), kind=kOutput, calls=%fused_computation.11 | convolution fusion | flops 1073741824 | bytes 12713984 | tf_op jit(solution)/shard_map/dot_general | solution.py:41
  27.0 0.0 reduce-scatter.4.cloned.1.call-update
  27.0 0.0 reduce-scatter.6.cloned.1.call-start
  27.1 66.6 %reduce-scatter.4.cloned.1.call-done = f32[8,8192]{1,0:T(8,128)} async-done(((f32[128,8192]{1,0:T(8,128)}), f32[8,8192]{1,0:T(8,128)}) %reduce-scatter.4.cloned.1.call-update) | async-done | bytes 262160 | tf_op jit(solution)/shard_map/reduce_scatter | solution.py:40
  93.6 0.0 copy-done.1
  93.7 1.0 fusion.4
  94.6 5.1 %collective-permute-start = (bf16[8,8192]{1,0:T(8,128)(2,1)S(1)}, bf16[8,8192]{1,0:T(8,128)(2,1)S(1)}, u32[]{:S(2)}, u32[]{:S(2)}) collective-permute-start(bf16[8,8192]{1,0:T(8,128)(2,1)S(1)} %fusion.4), channel_id=1, source_target_pairs={{0,240},{16,0},{32,16},{48,32},{64,48},{80,64},{96,80},{112,96},{1... | collective-permute-start | bytes 393224 | tf_op jit(solution)/shard_map/ppermute | solution.py:15
  99.7 1.9 collective-permute-done
  101.6 13.6 %all_to_all.33 = bf16[8,16,512]{2,0,1:T(8,128)(2,1)S(1)} all-to-all(bf16[8,16,512]{2,0,1:T(8,128)(2,1)S(1)} %bitcast.56), channel_id=1, replica_groups=mesh['section'=16,'dp'=16] {'dp'}, dimensions={1} | all-to-all | bytes 262144 | tf_op jit(solution)/shard_map/all_to_all | solution.py:39
  115.3 0.0 copy-start.2
  115.3 0.0 copy-start.3
  115.3 6.7 %fusion = f32[128,8192]{1,0:T(8,128)} fusion(bf16[1,512,8192]{2,1,0:T(8,128)(2,1)} %param.7, bf16[8,16,512]{2,0,1:T(8,128)(2,1)S(1)} %all_to_all.33), kind=kOutput, calls=%fused_computation.9 | convolution fusion | flops 1073741824 | bytes 12713984 | tf_op jit(solution)/shard_map/dot_general | solution.py:41
  122.0 0.0 reduce-scatter.6.cloned.1.call-update
  122.0 0.2 reduce-scatter.8.cloned.1.call-start
  122.3 0.0 copy-done.2
  122.3 0.6 gather_fusion.1
  122.9 0.6 gather_fusion.2
  123.4 0.0 copy-done.3
  123.5 4.9 %fusion.15 = f32[8,512,512]{2,1,0:T(8,128)} fusion(bf16[8,8,512]{2,1,0:T(8,128)(2,1)S(1)} %gather_fusion.2, pred[8]{0:T(512)(128)(4,1)S(1)} %get-tuple-element.7, bf16[8,8,512]{2,1,0:T(8,128)(2,1)S(1)} %gather_fusion.1, pred[8]{0:T(512)(128)(4,1)S(1)} %get-tuple-element.3), kind=kOutput, calls=%fused_computation.26 | convolution fusion | flops 33619968 | bytes 8519696 | tf_op jit(solution)/shard_map/tkb,tkc->kbc/dot_general | solution.py:25
  128.3 0.5 gather_fusion.3
  128.9 4.9 %fusion.13 = f32[8,512,512]{2,1,0:T(8,128)} fusion(bf16[8,8,512]{2,1,0:T(8,128)(2,1)S(1)} %gather_fusion.3, pred[8]{0:T(512)(128)(4,1)S(1)} %get-tuple-element.7, bf16[8,8,512]{2,1,0:T(8,128)(2,1)S(1)} %gather_fusion.1, pred[8]{0:T(512)(128)(4,1)S(1)} %get-tuple-element.3), kind=kOutput, calls=%fused_computation.24 | convolution fusion | flops 33619968 | bytes 8519696 | tf_op jit(solution)/shard_map/tkb,tkc->kbc/dot_general | solution.py:26
  133.7 0.5 gather_fusion.4
  134.3 0.6 gather_fusion.5
  134.9 4.9 %fusion.9 = f32[8,512,512]{2,1,0:T(8,128)} fusion(bf16[8,8,512]{2,1,0:T(8,128)(2,1)S(1)} %gather_fusion.5, pred[8]{0:T(512)(128)(4,1)S(1)} %get-tuple-element.7, bf16[8,8,512]{2,1,0:T(8,128)(2,1)S(1)} %gather_fusion.4, pred[8]{0:T(512)(128)(4,1)S(1)} %get-tuple-element.3), kind=kOutput, calls=%fused_computation.20 | convolution fusion | flops 33619968 | bytes 8519696 | tf_op jit(solution)/shard_map/tkb,tkc->kbc/dot_general | solution.py:25
  139.7 45.4 %reduce-scatter.6.cloned.1.call-done = f32[8,8192]{1,0:T(8,128)} async-done(((f32[128,8192]{1,0:T(8,128)}), f32[8,8192]{1,0:T(8,128)}) %reduce-scatter.6.cloned.1.call-update) | async-done | bytes 262160 | tf_op jit(solution)/shard_map/reduce_scatter | solution.py:40
  185.2 1.0 add_convert_fusion
  186.1 0.6 gather_fusion.6
  186.7 0.0 copy-start
  186.7 1.6 fusion.7
  188.3 1.7 copy-done
  190.1 12.7 %maximum_add_fusion = f32[16,512,512]{2,1,0:T(8,128)} fusion(f32[8,512,512]{2,1,0:T(8,128)} %fusion.13, f32[8,512,512]{2,1,0:T(8,128)} %fusion.15, f32[8,512,512]{2,1,0:T(8,128)S(1)} %fusion.7, f32[8,512,512]{2,1,0:T(8,128)S(1)} %copy-done), kind=kLoop, calls=%fused_computation.7 | loop fusion | flops 12582912 | bytes 50331648 | tf_op jit(solution)/shard_map/add | solution.py:47
  202.8 13.8 %gather_fusion = f32[16,512,512]{2,1,0:T(8,128)} fusion(f32[16,512,512]{2,1,0:T(8,128)} %maximum_add_fusion, s32[1024]{0:T(1024)S(1)} %pad_clamp_fusion), kind=kCustom, calls=%fused_computation.6 | custom fusion | bytes 33554496 | tf_op jit(solution)/shard_map/jit(_take)/gather | solution.py:49
  216.7 12.1 %select_multiply_fusion = f32[16,512,512]{2,1,0:T(8,128)} fusion(f32[16,512,512]{2,1,0:T(8,128)} %gather_fusion, pred[16]{0:T(512)(128)(4,1)S(1)} %compare_and_fusion.2), kind=kLoop, calls=%fused_computation.8 | loop fusion | flops 8388608 | bytes 33554448 | tf_op jit(solution)/shard_map/div | solution.py:49
  228.7 0.0 reduce-scatter.8.cloned.1.call-update
  228.8 5.3 %collective-permute-start.1 = (bf16[8,8192]{1,0:T(8,128)(2,1)S(1)}, bf16[8,8192]{1,0:T(8,128)(2,1)S(1)}, u32[]{:S(2)}, u32[]{:S(2)}) collective-permute-start(bf16[8,8192]{1,0:T(8,128)(2,1)S(1)} %add_convert_fusion), channel_id=1, source_target_pairs={{0,240},{16,0},{32,16},{48,32},{64,48},{80,64},{96,80},{112,96},{1... | collective-permute-start | bytes 393224 | tf_op jit(solution)/shard_map/ppermute | solution.py:15
  234.0 1.9 collective-permute-done.1
  236.0 94.4 %reduce-scatter.8.cloned.1.call-done = f32[1,512,512]{2,1,0:T(8,128)} async-done(((f32[16,512,512]{2,1,0:T(8,128)}), f32[1,512,512]{2,1,0:T(8,128)}) %reduce-scatter.8.cloned.1.call-update) | async-done | bytes 1048592 | tf_op jit(solution)/shard_map/reduce_scatter | solution.py:50
  330.4 0.7 copy.7
  (5 shorter events, 0.0 us)
Async XLA Ops:
  7.2 86.5 %reduce-scatter.4.cloned.1.call-start = ((), (), s32[]{:S(2)}) async-start(), calls=%async_computation.5 | async-start | bytes 4456448 | tf_op jit(solution)/shard_map/reduce_scatter | solution.py:40
  20.3 73.4 %copy-start.1 = (bf16[1,8,8192]{2,1,0:T(8,128)(2,1)S(1)}, bf16[1,8,8192]{2,1,0:T(8,128)(2,1)}, u32[]{:S(2)}) copy-start(bf16[1,8,8192]{2,1,0:T(8,128)(2,1)} %param.6) | copy-start | bytes 393220
  27.0 158.1 %reduce-scatter.6.cloned.1.call-start = ((), (), s32[]{:S(2)}) async-start(), calls=%async_computation.6 | async-start | bytes 4456448 | tf_op jit(solution)/shard_map/reduce_scatter | solution.py:40
  94.6 7.0 %collective-permute-start = (bf16[8,8192]{1,0:T(8,128)(2,1)S(1)}, bf16[8,8192]{1,0:T(8,128)(2,1)S(1)}, u32[]{:S(2)}, u32[]{:S(2)}) collective-permute-start(bf16[8,8192]{1,0:T(8,128)(2,1)S(1)} %fusion.4), channel_id=1, source_target_pairs={{0,240},{16,0},{32,16},{48,32},{64,48},{80,64},{96,80},{112,96},{1... | collective-permute-start | bytes 393224 | tf_op jit(solution)/shard_map/ppermute | solution.py:15
  115.3 7.0 %copy-start.2 = (s32[1,8,2]{1,2,0:T(2,128)S(1)}, s32[1,8,2]{1,2,0:T(2,128)}, u32[]{:S(2)}) copy-start(s32[1,8,2]{1,2,0:T(2,128)} %param.8) | copy-start | bytes 196
  115.3 8.2 %copy-start.3 = (s32[16]{0:T(128)S(1)}, s32[16]{0:T(128)}, u32[]{:S(2)}) copy-start(s32[16]{0:T(128)} %param.9) | copy-start | bytes 196
  122.0 208.3 %reduce-scatter.8.cloned.1.call-start = ((), (), s32[]{:S(2)}) async-start(), calls=%async_computation.7 | async-start | bytes 17825792 | tf_op jit(solution)/shard_map/reduce_scatter | solution.py:50
  186.7 3.4 %copy-start = (f32[8,512,512]{2,1,0:T(8,128)S(1)}, f32[8,512,512]{2,1,0:T(8,128)}, u32[]{:S(2)}) copy-start(f32[8,512,512]{2,1,0:T(8,128)} %fusion.9) | copy-start | bytes 25165828
  228.8 7.2 %collective-permute-start.1 = (bf16[8,8192]{1,0:T(8,128)(2,1)S(1)}, bf16[8,8192]{1,0:T(8,128)(2,1)S(1)}, u32[]{:S(2)}, u32[]{:S(2)}) collective-permute-start(bf16[8,8192]{1,0:T(8,128)(2,1)S(1)} %add_convert_fusion), channel_id=1, source_target_pairs={{0,240},{16,0},{32,16},{48,32},{64,48},{80,64},{96,80},{112,96},{1... | collective-permute-start | bytes 393224 | tf_op jit(solution)/shard_map/ppermute | solution.py:15
Sparse Core Ops, SparseCore 0:
  27.1 66.4 reduce-scatter.3
  122.2 62.9 reduce-scatter.5
  228.9 101.4 reduce-scatter.7
where the time goes:
time: 338 us
  waiting for transfers between devices  210 us (62%)
  matrix products  29.7 us (9%)
  other arithmetic  26.8 us (8%)
  blocking collectives  26.7 us (8%)
  local copies, waits for them, and re-layouts  19.6 us (6%)
  between operations  13.9 us (4%)
  starting transfers between devices  10.6 us (3%)
    reduce_scatter x2, waiting for transfers between devices, shards(): lax.psum_scatter(jnp.dot(banded, w_rows, preferred_element_type=jnp.float...  112 us
    reduce_scatter x1, waiting for transfers between devices, shards(): owned = lax.psum_scatter(ordered, 'dp', scatter_dimension=0, tiled=True)  94.4 us
    all_to_all x2, blocking collectives, shards(): banded = lax.all_to_all(held, 'dp', split_axis=1, concat_axis=0, tiled=True)  26.7 us
    gather x1, local copies, waits for them, and re-layouts, shards(): ordered = jnp.take(totals, owner, axis=0) / float(all_tokens * STEPS)  13.8 us
    dot_general x2, matrix products, shards(): jnp.dot(banded, w_rows, preferred_element_type=jnp.float32)  13.5 us
    add x1, other arithmetic, shards(): totals = totals + gram_blocks(held, fresh, pairs)  12.7 us
    div x1, other arithmetic, shards(): ordered = jnp.take(totals, owner, axis=0) / float(all_tokens * STEPS)  12.1 us
    ppermute x2, starting transfers between devices, passed_along(): return lax.ppermute(value, axis, pairs)  10.3 us
  transfers between devices with their start and end apart: 5, of which 5 were waited for; matrix products, arithmetic and copies ran while one was open for 5% of the time, Pallas kernels for 0%

commit v1 on v0

v1 whole, which is shorter than its diff:
```python
import functools

import jax
import jax.numpy as jnp
from jax import lax
from jax.experimental import pallas as pl
from jax.experimental.pallas import tpu as pltpu
from jax.sharding import PartitionSpec as P

D = 8192
BLK = 512
HALF = 256
NB = 8
STEPS = 2
TOKENS = 128
DP = 16
CHIPS = 8
TOK = TOKENS // DP
ROWS = 2 * TOK
BANDS = D // BLK
CHUNKS = 4
PER = BANDS // CHUNKS
MESH = pl.DeviceIdType.MESH
F32 = jnp.float32
BF16 = jnp.bfloat16

ROUTES = (
    ((1, 2), (1, 0), 4, ()),
    ((1, 1), (0, 1), 5, ()),
    ((1, 3), (0, 3), 6, ()),
    ((0, 1), (0, 1), 0, ()),
    ((0, 3), (0, 3), 1, ()),
    ((0, 2), (0, 2), 2, (4,)),
    ((1, 0), (1, 0), 3, (5, 6)),
    ((0, 0), None, None, ()),
)
SLOTS = 7
FINAL = 4


def folded(rows):
    cut = rows.reshape(rows.shape[0] // TOK, TOK, BLK)
    return jnp.concatenate([cut[:, :, :HALF], cut[:, :, HALF:]], axis=1)


def unfolded(blocks):
    wide = blocks.astype(F32)
    flat = jnp.concatenate([wide[:, :TOK], wide[:, TOK:]], axis=2)
    return flat.reshape(blocks.shape[0] * TOK, BLK)


def kernel(
    g_ref, w_hbm, band_ref, owner_ref, factors_ref, gout_ref,
    w, gtok, banded, x0, x1_out, x1,
    sib_out0, sib_in0, own0, rs_out0, rs_in0,
    sib_out1, sib_in1, own1, rs_out1, rs_in1,
    n0_out, right0, g1tok, right1, gout_in,
    l0_out, r0_out, l1_out, r1_out, l0_in, r0_in, l1_in, r1_in,
    w_sem, a2a_send, a2a_recv, sib_send0, sib_recv0, sib_send1, sib_recv1,
    rs_send0, rs_recv0, rs_send1, rs_recv1, pass_send, pass_recv, go_send, go_recv,
):
    sec = lax.axis_index("section")
    me = lax.axis_index("dp")
    secs = lax.axis_size("section")
    core = me % 2
    y = (me // 2) % 4
    x = me // 8
    before = (sec + secs - 1) % secs
    after = (sec + 1) % secs

    def chip(dx, dy):
        return ((x + dx) % 2) * 4 + (y + dy) % 4

    def peer(r):
        return chip(r // 8, (r // 2) % 4) * 2 + (core + r) % 2

    def remote(src, dst, send, recv, device):
        return pltpu.make_async_remote_copy(
            src_ref=src, dst_ref=dst, send_sem=send, recv_sem=recv,
            device_id=device, device_id_type=MESH,
        )

    def w_copy(k):
        cols = pl.ds(pl.multiple_of(chip(*ROUTES[k][0]) * 2 * BLK, 2 * BLK), 2 * BLK)
        return pltpu.make_async_copy(w_hbm.at[:, cols], w.at[:, cols], w_sem.at[k])

    for k in range(CHIPS):
        w_copy(k).start()

    barrier = pltpu.get_barrier_semaphore()

    def greet(r, carry):
        pl.semaphore_signal(barrier, inc=1, device_id=(sec, peer(r)), device_id_type=MESH)
        return carry

    lax.fori_loop(1, DP, greet, 0)
    pl.semaphore_signal(barrier, inc=1, device_id=(before, me), device_id_type=MESH)
    pl.semaphore_signal(barrier, inc=1, device_id=(after, me), device_id_type=MESH)

    wide = g_ref[...].astype(F32)
    for b in range(BANDS):
        gtok[b] = folded(wide[:, b * BLK:(b + 1) * BLK])[0].astype(BF16)

    pl.semaphore_wait(barrier, DP + 1)

    def exchange(which, out, into, base=0):
        def copy(r):
            q = peer(r)
            return remote(out.at[q], into.at[base + me], a2a_send.at[which, r], a2a_recv.at[which, r], (sec, q))

        def start():
            def body(r, carry):
                copy(r).start()
                return carry
            lax.fori_loop(1, DP, body, 0)
            into[base + me] = out[me]

        def recv():
            def body(r, carry):
                copy(r).wait_recv()
                return carry
            lax.fori_loop(1, DP, body, 0)

        def sent():
            def body(r, carry):
                copy(r).wait_send()
                return carry
            lax.fori_loop(1, DP, body, 0)

        return start, recv, sent

    a_start, a_recv, a_sent = exchange(0, gtok, banded)
    n_start, n_recv, n_sent = exchange(1, n0_out, right0, BANDS)
    l0_start, l0_recv, l0_sent = exchange(2, l0_out, l0_in)
    r0_start, r0_recv, r0_sent = exchange(3, r0_out, r0_in)
    l1_start, l1_recv, l1_sent = exchange(4, l1_out, l1_in)
    r1_start, r1_recv, r1_sent = exchange(5, r1_out, r1_in)

    a_start()

    def select(out, source, column):
        def body(q, carry):
            slot = owner_ref[q]
            k = slot % NB
            index = band_ref[k, column]
            if column == 1:
                index = index + (slot // NB) * BANDS
            out[q] = source[index]
            return carry
        lax.fori_loop(0, DP, body, 0)

    select(l0_out, gtok, 0)
    right0[:BANDS] = gtok[...]

    a_recv()
    x0[...] = unfolded(banded[...]).astype(BF16)

    def sibling0(k):
        return remote(sib_out0.at[k], sib_in0.at[k], sib_send0.at[k], sib_recv0.at[k], (sec, chip(0, 0) * 2 + 1 - core))

    def rs0(k):
        _, to, slot, _ = ROUTES[k]
        return remote(rs_out0.at[k], rs_in0.at[slot], rs_send0.at[k], rs_recv0.at[slot], (sec, chip(*to) * 2 + core))

    def arrived0(slot):
        k = [r[2] for r in ROUTES].index(slot)
        rs0(k).wait_recv()
        return rs_in0[slot].astype(F32)

    def compute0(k):
        m = chip(*ROUTES[k][0])
        w_copy(k).wait()
        other = pl.ds(pl.multiple_of((m * 2 + 1 - core) * BLK, BLK), BLK)
        mine = pl.ds(pl.multiple_of((m * 2 + core) * BLK, BLK), BLK)
        sib_out0[k] = jnp.dot(x0[...], w[:, other], preferred_element_type=F32).astype(BF16)
        sibling0(k).start()
        own0[k] = jnp.dot(x0[...], w[:, mine], preferred_element_type=F32)

    def finish0(k):
        sibling0(k).wait_recv()
        total = own0[k] + sib_in0[k].astype(F32)
        for slot in ROUTES[k][3]:
            total = total + arrived0(slot)
        if k < CHIPS - 1:
            rs_out0[k] = total.astype(BF16)
            rs0(k).start()
        else:
            own0[k] = total

    for k in range(CHIPS):
        compute0(k)
        if k > 0:
            finish0(k - 1)
    finish0(CHIPS - 1)
    total = own0[CHIPS - 1] + x0[...].astype(F32)
    for slot in range(FINAL):
        total = total + arrived0(slot)

    by_core = total.reshape(CHIPS, 2, TOK, BLK)
    first = core == 0
    x1_out[:TOKENS // 2] = jnp.where(first, by_core[:, 1], by_core[:, 0]).reshape(TOKENS // 2, BLK).astype(BF16)
    x1_out[TOKENS // 2:] = jnp.where(first, by_core[:, 0], by_core[:, 1]).reshape(TOKENS // 2, BLK).astype(BF16)
    band_pass = remote(x1_out, x1, pass_send.at[0], pass_recv.at[0], (before, me))
    band_pass.start()
    n0_out[...] = folded(total).astype(BF16)
    n_start()
    l0_start()

    token_pass = remote(right0.at[pl.ds(BANDS, BANDS)], g1tok, pass_send.at[1], pass_recv.at[1], (before, me))
    n_recv()
    token_pass.start()
    select(r0_out, right0, 1)
    r0_start()

    def sibling1(j):
        return remote(sib_out1.at[j], sib_in1.at[j], sib_send1.at[j], sib_recv1.at[j], (sec, chip(0, 0) * 2 + 1 - core))

    def rs1(j, k):
        _, to, slot, _ = ROUTES[k]
        return remote(rs_out1.at[j, k], rs_in1.at[j, slot], rs_send1.at[j, k], rs_recv1.at[j, slot], (sec, chip(*to) * 2 + core))

    def arrived1(j, slot):
        k = [r[2] for r in ROUTES].index(slot)
        rs1(j, k).wait_recv()
        return rs_in1[j, slot].astype(F32)

    def compute1(j):
        for e in range(PER):
            band = j * PER + e
            part = jnp.dot(x1[...], w[:, band * BLK:(band + 1) * BLK], preferred_element_type=F32)
            sib_out1[j, :, e] = folded(part[:TOKENS // 2]).astype(BF16)
            own1[j, :, e] = folded(part[TOKENS // 2:])
        sibling1(j).start()

    def finish1(j, ks):
        for k in ks:
            m = chip(*ROUTES[k][0])
            total = own1[j, m] + sib_in1[j, m].astype(F32)
            for slot in ROUTES[k][3]:
                total = total + arrived1(j, slot)
            rs_out1[j, k] = total.astype(BF16)
            rs1(j, k).start()

    def early1(j):
        sibling1(j).wait_recv()
        finish1(j, (0, 1, 2, 3, 4))

    def late1(j):
        finish1(j, (5, 6))

    def gout_copy(j):
        return remote(
            right1.at[pl.ds(BANDS + j * PER, PER)], gout_in.at[pl.ds(j * PER, PER)],
            go_send.at[j], go_recv.at[j], (before, me),
        )

    def last1(j):
        total = own1[j, chip(0, 0)] + sib_in1[j, chip(0, 0)].astype(F32)
        total = total + g1tok[j * PER:(j + 1) * PER].astype(F32)
        for slot in range(FINAL):
            total = total + arrived1(j, slot)
        right1[BANDS + j * PER:BANDS + (j + 1) * PER] = total.astype(BF16)
        gout_copy(j).start()

    band_pass.wait_recv()
    compute1(0)
    compute1(1)
    early1(0)
    compute1(2)
    early1(1)
    late1(0)
    compute1(3)
    early1(2)
    late1(1)
    early1(3)
    late1(2)
    late1(3)
    token_pass.wait_recv()
    select(l1_out, g1tok, 0)
    l1_start()
    right1[:BANDS] = g1tok[...]
    for j in range(CHUNKS):
        last1(j)
    select(r1_out, right1, 1)
    r1_start()

    def gram(left, right):
        return lax.dot_general(
            unfolded(left[...]).astype(BF16), unfolded(right[...]).astype(BF16),
            (((0,), (0,)), ((), ())), preferred_element_type=F32,
        )

    l0_recv()
    r0_recv()
    factors_ref[...] = gram(l0_in, r0_in)
    for j in range(CHUNKS):
        gout_copy(j).wait_recv()
    for b in range(BANDS):
        gout_ref[:, b * BLK:(b + 1) * BLK] = unfolded(gout_in[b:b + 1]).astype(BF16)
    l1_recv()
    r1_recv()
    factors_ref[...] = (factors_ref[...] + gram(l1_in, r1_in)) * (1.0 / (TOKENS * STEPS))

    a_sent()
    n_sent()
    l0_sent()
    r0_sent()
    l1_sent()
    r1_sent()
    band_pass.wait_send()
    token_pass.wait_send()
    for k in range(CHIPS):
        sibling0(k).wait_send()
        if k < CHIPS - 1:
            rs0(k).wait_send()
    for j in range(CHUNKS):
        sibling1(j).wait_send()
        gout_copy(j).wait_send()
        for k in range(CHIPS - 1):
            rs1(j, k).wait_send()


def shards(grad_in, weights, band_index, owner):
    vmem = pl.BlockSpec(memory_space=pltpu.VMEM)
    smem = pl.BlockSpec(memory_space=pltpu.SMEM)
    tok = (BANDS, ROWS, HALF)
    dma = pltpu.SemaphoreType.DMA
    factors, gout = pl.pallas_call(
        kernel,
        out_shape=(
            jax.ShapeDtypeStruct((BLK, BLK), F32),
            jax.ShapeDtypeStruct((TOK, D), BF16),
        ),
        in_specs=[vmem, pl.BlockSpec(memory_space=pl.ANY), smem, smem],
        out_specs=(vmem, vmem),
        scratch_shapes=[
            pltpu.VMEM((BLK, D), BF16),
            pltpu.VMEM(tok, BF16),
            pltpu.VMEM(tok, BF16),
            pltpu.VMEM((TOKENS, BLK), BF16),
            pltpu.VMEM((TOKENS, BLK), BF16),
            pltpu.VMEM((TOKENS, BLK), BF16),
            pltpu.VMEM((CHIPS, TOKENS, BLK), BF16),
            pltpu.VMEM((CHIPS, TOKENS, BLK), BF16),
            pltpu.VMEM((CHIPS, TOKENS, BLK), F32),
            pltpu.VMEM((SLOTS, TOKENS, BLK), BF16),
            pltpu.VMEM((SLOTS, TOKENS, BLK), BF16),
            pltpu.VMEM((CHUNKS, CHIPS, PER, ROWS, HALF), BF16),
            pltpu.VMEM((CHUNKS, CHIPS, PER, ROWS, HALF), BF16),
            pltpu.VMEM((CHUNKS, CHIPS, PER, ROWS, HALF), F32),
            pltpu.VMEM((CHUNKS, SLOTS, PER, ROWS, HALF), BF16),
            pltpu.VMEM((CHUNKS, SLOTS, PER, ROWS, HALF), BF16),
            pltpu.VMEM(tok, BF16),
            pltpu.VMEM((2 * BANDS, ROWS, HALF), BF16),
            pltpu.VMEM(tok, BF16),
            pltpu.VMEM((2 * BANDS, ROWS, HALF), BF16),
            pltpu.VMEM(tok, BF16),
        ] + [pltpu.VMEM(tok, BF16)] * 8 + [
            dma((CHIPS,)),
            dma((6, DP)),
            dma((6, DP)),
            dma((CHIPS,)),
            dma((CHIPS,)),
            dma((CHUNKS,)),
            dma((CHUNKS,)),
            dma((SLOTS,)),
            dma((SLOTS,)),
            dma((CHUNKS, SLOTS)),
            dma((CHUNKS, SLOTS)),
            dma((2,)),
            dma((2,)),
            dma((CHUNKS,)),
            dma((CHUNKS,)),
        ],
        compiler_params=pltpu.CompilerParams(
            collective_id=0, has_side_effects=True, vmem_limit_bytes=40 * 2 ** 20,
        ),
        name="relay",
    )(grad_in[0], weights[0], band_index[0], owner)
    return factors[None, None], gout[None]


def solution(mesh):
    return jax.shard_map(
        shards,
        mesh=mesh,
        in_specs=(
            P("section", "dp", None),
            P("section", "dp", None),
            P("section", None, None),
            P(),
        ),
        out_specs=(P("section", "dp", None, None), P("section", "dp", None)),
        check_vma=False,
    )
```

time: 338 us -> 67.7 us (0.20)
  waiting for transfers between devices: 210 us -> 0 us
  Pallas kernels: 0 us -> 59.6 us
  matrix products: 29.7 us -> 0 us
  other arithmetic: 26.8 us -> 0 us
  blocking collectives: 26.7 us -> 0 us
  between operations: 13.9 us -> 0.64 us
  local copies, waits for them, and re-layouts: 19.6 us -> 7.32 us
  starting transfers between devices: 10.6 us -> 0 us
    reduce_scatter x3 -> x0, waiting for transfers between devices: 206 us -> none  [the longest x2 112 us: shards(): lax.psum_scatter(jnp.dot(banded, w_rows, preferred_element_type=jnp.float...]
    pallas_call x0 -> x1, Pallas kernels: none -> 59.6 us  [shards(): pl.pallas_call(kernel, out_shape=(jax.ShapeDtypeStruct((BLK, BLK), F32),...]
    dot_general x6 -> x0, matrix products: 29.7 us -> none  [the longest x2 13.5 us: shards(): jnp.dot(banded, w_rows, preferred_element_type=jnp.float32)]
    all_to_all x2 -> x0, blocking collectives: 26.7 us -> none  [shards(): banded = lax.all_to_all(held, 'dp', split_axis=1, concat_axis=0, tiled=True)]
    gather x7 -> x0, local copies, waits for them, and re-layouts: 17.1 us -> none  [the longest x1 13.8 us: shards(): ordered = jnp.take(totals, owner, axis=0) / float(all_tokens * STEPS)]
    add x1 -> x0, other arithmetic: 12.7 us -> none  [shards(): totals = totals + gram_blocks(held, fresh, pairs)]
    div x1 -> x0, other arithmetic: 12.1 us -> none  [shards(): ordered = jnp.take(totals, owner, axis=0) / float(all_tokens * STEPS)]
    ppermute x2 -> x0, starting transfers between devices: 10.3 us -> none  [passed_along(): return lax.ppermute(value, axis, pairs)]
  transfers between devices with their start and end apart: 5 -> 0, of which waited for: 5 -> 0; matrix products, arithmetic and copies ran while one was open for 5% -> 0% of each run, Pallas kernels for 0% -> 0%
where the time goes in v1:
time: 67.7 us; the launch traced here: 67.6 us
  Pallas kernels  59.6 us (88%)
  local copies, waits for them, and re-layouts  7.32 us (11%)
    pallas_call x1, Pallas kernels, shards(): pl.pallas_call(kernel, out_shape=(jax.ShapeDtypeStruct((BLK, BLK), F32),...  59.6 us
    unnamed x8, local copies, waits for them, and re-layouts  6.57 us

profile of v1, /device:TPU:1, one launch (start us, length us, event | category | flops | bytes accessed | tf_op | source)
XLA Modules:
  0.0 67.6 jit_solution(15775697090027885926)
XLA Ops:
  0.6 0.8 %copy.6.band_ref = s32[8,2]{1,0:T(8,128)S(1)} copy(s32[8,2]{0,1:T(2,128)} %bitcast.9) | data formatting | bytes 128 | tf_op jit(solution)/shard_map/squeeze | solution.py:379
  1.4 0.0 copy-start
  1.4 3.4 %copy-done = bf16[1,512,8192]{2,1,0:T(8,128)(2,1)S(1)} copy-done((bf16[1,512,8192]{2,1,0:T(8,128)(2,1)S(1)}, bf16[1,512,8192]{2,1,0:T(8,128)(2,1)}, u32[]{:S(2)}) %copy-start) | copy-done | bytes 8388632
  4.8 0.0 copy-start.1
  4.8 0.9 %copy-done.1 = bf16[1,8,8192]{2,1,0:T(8,128)(2,1)S(1)} copy-done((bf16[1,8,8192]{2,1,0:T(8,128)(2,1)S(1)}, bf16[1,8,8192]{2,1,0:T(8,128)(2,1)}, u32[]{:S(2)}) %copy-start.1) | copy-done | bytes 131096
  5.7 0.0 copy-start.2
  5.7 0.7 copy-done.2
  6.3 59.6 %relay.1 = (f32[512,512]{1,0:T(8,128)S(1)}, bf16[8,8192]{1,0:T(8,128)(2,1)S(1)}) custom-call(bf16[8,8192]{1,0:T(8,128)(2,1)S(1)} %bitcast.7, bf16[512,8192]{1,0:T(8,128)(2,1)S(1)} %bitcast.5, s32[8,2]{1,0:T(8,128)S(1)} %copy.6.band_ref, s32[16]{0:T(128)S(1)} %copy-done.2), custom_call_target="tpu_custom_call" | custom-call | tf_op jit(solution)/shard_map/relay/pallas_call | solution.py:328
  66.0 1.0 %copy.9 = f32[1,1,512,512]{3,2,1,0:T(8,128)} copy(f32[1,1,512,512]{3,2,1,0:T(8,128)S(1)} %bitcast.6) | data formatting | bytes 2097152
  66.9 0.7 copy.10
Async XLA Ops:
  1.4 3.4 %copy-start = (bf16[1,512,8192]{2,1,0:T(8,128)(2,1)S(1)}, bf16[1,512,8192]{2,1,0:T(8,128)(2,1)}, u32[]{:S(2)}) copy-start(bf16[1,512,8192]{2,1,0:T(8,128)(2,1)} %param.5) | copy-start | bytes 25165828
  4.8 0.9 %copy-start.1 = (bf16[1,8,8192]{2,1,0:T(8,128)(2,1)S(1)}, bf16[1,8,8192]{2,1,0:T(8,128)(2,1)}, u32[]{:S(2)}) copy-start(bf16[1,8,8192]{2,1,0:T(8,128)(2,1)} %param.4) | copy-start | bytes 393220
  5.7 0.7 copy-start.2

commit v2 on v1

--- a/solution.py
+++ b/solution.py
@@ -25,9 +25,9 @@
 BF16 = jnp.bfloat16
 
 ROUTES = (
-    ((1, 2), (1, 0), 4, ()),
     ((1, 1), (0, 1), 5, ()),
     ((1, 3), (0, 3), 6, ()),
+    ((1, 2), (1, 0), 4, ()),
     ((0, 1), (0, 1), 0, ()),
     ((0, 3), (0, 3), 1, ()),
     ((0, 2), (0, 2), 2, (4,)),
@@ -35,6 +35,11 @@
     ((0, 0), None, None, ()),
 )
 SLOTS = 7
+PEERS = tuple(
+    (dx, dy, dc)
+    for dx, dy in ((1, 2), (1, 1), (1, 3), (0, 2), (1, 0), (0, 1), (0, 3), (0, 0))
+    for dc in ((1, 0) if (dx, dy) != (0, 0) else (1,))
+)
 FINAL = 4
 
 
@@ -50,13 +55,13 @@
 
 
 def kernel(
-    g_ref, w_hbm, band_ref, owner_ref, factors_ref, gout_ref,
-    w, gtok, banded, x0, x1_out, x1,
+    g_hbm, w_hbm, band_hbm, owner_hbm, factors_ref, gout_ref,
+    g_ref, band_ref, owner_ref, w, gtok, banded, x0, x1_out, x1,
     sib_out0, sib_in0, own0, rs_out0, rs_in0,
     sib_out1, sib_in1, own1, rs_out1, rs_in1,
     n0_out, right0, g1tok, right1, gout_in,
     l0_out, r0_out, l1_out, r1_out, l0_in, r0_in, l1_in, r1_in,
-    w_sem, a2a_send, a2a_recv, sib_send0, sib_recv0, sib_send1, sib_recv1,
+    in_sem, w_sem, a2a_send, a2a_recv, sib_send0, sib_recv0, sib_send1, sib_recv1,
     rs_send0, rs_recv0, rs_send1, rs_recv1, pass_send, pass_recv, go_send, go_recv,
 ):
     sec = lax.axis_index("section")
@@ -68,11 +73,16 @@
     before = (sec + secs - 1) % secs
     after = (sec + 1) % secs
 
+    xs = (x, 1 - x)
+    ys = tuple((y + d) % 4 for d in range(4))
+    chips = {(dx, dy): xs[dx] * 4 + ys[dy] for dx in range(2) for dy in range(4)}
+
     def chip(dx, dy):
-        return ((x + dx) % 2) * 4 + (y + dy) % 4
+        return chips[dx, dy]
 
     def peer(r):
-        return chip(r // 8, (r // 2) % 4) * 2 + (core + r) % 2
+        dx, dy, dc = PEERS[r]
+        return chips[dx, dy] * 2 + (core if dc == 0 else 1 - core)
 
     def remote(src, dst, send, recv, device):
         return pltpu.make_async_remote_copy(
@@ -84,19 +94,21 @@
         cols = pl.ds(pl.multiple_of(chip(*ROUTES[k][0]) * 2 * BLK, 2 * BLK), 2 * BLK)
         return pltpu.make_async_copy(w_hbm.at[:, cols], w.at[:, cols], w_sem.at[k])
 
+    barrier = pltpu.get_barrier_semaphore()
+    for r in range(DP - 1):
+        pl.semaphore_signal(barrier, inc=1, device_id=(sec, peer(r)), device_id_type=MESH)
+    pl.semaphore_signal(barrier, inc=1, device_id=(before, me), device_id_type=MESH)
+    pl.semaphore_signal(barrier, inc=1, device_id=(after, me), device_id_type=MESH)
+
+    g_in = pltpu.make_async_copy(g_hbm, g_ref, in_sem.at[0])
+    band_in = pltpu.make_async_copy(band_hbm, band_ref, in_sem.at[1])
+    owner_in = pltpu.make_async_copy(owner_hbm, owner_ref, in_sem.at[2])
+    g_in.start()
+    band_in.start()
+    owner_in.start()
     for k in range(CHIPS):
         w_copy(k).start()
-
-    barrier = pltpu.get_barrier_semaphore()
-
-    def greet(r, carry):
-        pl.semaphore_signal(barrier, inc=1, device_id=(sec, peer(r)), device_id_type=MESH)
-        return carry
-
-    lax.fori_loop(1, DP, greet, 0)
-    pl.semaphore_signal(barrier, inc=1, device_id=(before, me), device_id_type=MESH)
-    pl.semaphore_signal(barrier, inc=1, device_id=(after, me), device_id_type=MESH)
-
+    g_in.wait()
     wide = g_ref[...].astype(F32)
     for b in range(BANDS):
         gtok[b] = folded(wide[:, b * BLK:(b + 1) * BLK])[0].astype(BF16)
@@ -109,23 +121,17 @@
             return remote(out.at[q], into.at[base + me], a2a_send.at[which, r], a2a_recv.at[which, r], (sec, q))
 
         def start():
-            def body(r, carry):
+            for r in range(DP - 1):
                 copy(r).start()
-                return carry
-            lax.fori_loop(1, DP, body, 0)
             into[base + me] = out[me]
 
         def recv():
-            def body(r, carry):
+            for r in reversed(range(DP - 1)):
                 copy(r).wait_recv()
-                return carry
-            lax.fori_loop(1, DP, body, 0)
 
         def sent():
-            def body(r, carry):
+            for r in range(DP - 1):
                 copy(r).wait_send()
-                return carry
-            lax.fori_loop(1, DP, body, 0)
 
         return start, recv, sent
 
@@ -137,20 +143,16 @@
     r1_start, r1_recv, r1_sent = exchange(5, r1_out, r1_in)
 
     a_start()
+    band_in.wait()
+    owner_in.wait()
 
     def select(out, source, column):
-        def body(q, carry):
+        for q in range(DP):
             slot = owner_ref[q]
-            k = slot % NB
-            index = band_ref[k, column]
+            index = band_ref[column, slot % NB]
             if column == 1:
                 index = index + (slot // NB) * BANDS
             out[q] = source[index]
-            return carry
-        lax.fori_loop(0, DP, body, 0)
-
-    select(l0_out, gtok, 0)
-    right0[:BANDS] = gtok[...]
 
     a_recv()
     x0[...] = unfolded(banded[...]).astype(BF16)
@@ -167,13 +169,16 @@
         rs0(k).wait_recv()
         return rs_in0[slot].astype(F32)
 
-    def compute0(k):
+    def other0(k):
         m = chip(*ROUTES[k][0])
         w_copy(k).wait()
         other = pl.ds(pl.multiple_of((m * 2 + 1 - core) * BLK, BLK), BLK)
-        mine = pl.ds(pl.multiple_of((m * 2 + core) * BLK, BLK), BLK)
         sib_out0[k] = jnp.dot(x0[...], w[:, other], preferred_element_type=F32).astype(BF16)
         sibling0(k).start()
+
+    def mine0(k):
+        m = chip(*ROUTES[k][0])
+        mine = pl.ds(pl.multiple_of((m * 2 + core) * BLK, BLK), BLK)
         own0[k] = jnp.dot(x0[...], w[:, mine], preferred_element_type=F32)
 
     def finish0(k):
@@ -187,11 +192,12 @@
         else:
             own0[k] = total
 
+    other0(0)
     for k in range(CHIPS):
-        compute0(k)
-        if k > 0:
-            finish0(k - 1)
-    finish0(CHIPS - 1)
+        if k + 1 < CHIPS:
+            other0(k + 1)
+        mine0(k)
+        finish0(k)
     total = own0[CHIPS - 1] + x0[...].astype(F32)
     for slot in range(FINAL):
         total = total + arrived0(slot)
@@ -204,13 +210,11 @@
     band_pass.start()
     n0_out[...] = folded(total).astype(BF16)
     n_start()
+    select(l0_out, gtok, 0)
     l0_start()
+    right0[:BANDS] = gtok[...]
 
     token_pass = remote(right0.at[pl.ds(BANDS, BANDS)], g1tok, pass_send.at[1], pass_recv.at[1], (before, me))
-    n_recv()
-    token_pass.start()
-    select(r0_out, right0, 1)
-    r0_start()
 
     def sibling1(j):
         return remote(sib_out1.at[j], sib_in1.at[j], sib_send1.at[j], sib_recv1.at[j], (sec, chip(0, 0) * 2 + 1 - core))
@@ -266,9 +270,13 @@
     compute1(0)
     compute1(1)
     early1(0)
+    n_recv()
+    token_pass.start()
     compute1(2)
     early1(1)
     late1(0)
+    select(r0_out, right0, 1)
+    r0_start()
     compute1(3)
     early1(2)
     late1(1)
@@ -322,18 +330,20 @@
 
 def shards(grad_in, weights, band_index, owner):
     vmem = pl.BlockSpec(memory_space=pltpu.VMEM)
-    smem = pl.BlockSpec(memory_space=pltpu.SMEM)
     tok = (BANDS, ROWS, HALF)
     dma = pltpu.SemaphoreType.DMA
     factors, gout = pl.pallas_call(
         kernel,
         out_shape=(
-            jax.ShapeDtypeStruct((BLK, BLK), F32),
-            jax.ShapeDtypeStruct((TOK, D), BF16),
+            pltpu.VMEM((BLK, BLK), F32),
+            pltpu.VMEM((TOK, D), BF16),
         ),
-        in_specs=[vmem, pl.BlockSpec(memory_space=pl.ANY), smem, smem],
+        in_specs=[pl.BlockSpec(memory_space=pl.ANY)] * 4,
         out_specs=(vmem, vmem),
         scratch_shapes=[
+            pltpu.VMEM((TOK, D), BF16),
+            pltpu.SMEM((2, NB), jnp.int32),
+            pltpu.SMEM((DP,), jnp.int32),
             pltpu.VMEM((BLK, D), BF16),
             pltpu.VMEM(tok, BF16),
             pltpu.VMEM(tok, BF16),
@@ -356,6 +366,7 @@
             pltpu.VMEM((2 * BANDS, ROWS, HALF), BF16),
             pltpu.VMEM(tok, BF16),
         ] + [pltpu.VMEM(tok, BF16)] * 8 + [
+            dma((3,)),
             dma((CHIPS,)),
             dma((6, DP)),
             dma((6, DP)),
@@ -373,10 +384,10 @@
             dma((CHUNKS,)),
         ],
         compiler_params=pltpu.CompilerParams(
-            collective_id=0, has_side_effects=True, vmem_limit_bytes=40 * 2 ** 20,
+            collective_id=0, has_side_effects=True, vmem_limit_bytes=58 * 2 ** 20,
         ),
         name="relay",
-    )(grad_in[0], weights[0], band_index[0], owner)
+    )(grad_in[0], weights[0], band_index[0].T, owner)
     return factors[None, None], gout[None]
 
 

time: 67.7 us -> 57.3 us (0.85)
  the two profiles are of different devices: /device:TPU:1 before, /device:TPU:224 now
where the time goes in v2:
time: 57.3 us; the launch traced here: 57.2 us
  Pallas kernels  55 us (96%)
  local copies, waits for them, and re-layouts  1.63 us (3%)
  between operations  0.64 us (1%)
    pallas_call x1, Pallas kernels, shards(): pl.pallas_call(kernel, out_shape=(pltpu.VMEM((BLK, BLK), F32), pltpu.VMEM...  55 us
    unnamed x2, local copies, waits for them, and re-layouts  1.63 us

profile of v2, /device:TPU:224, one launch (start us, length us, event | category | flops | bytes accessed | tf_op | source)
XLA Modules:
  0.0 57.2 jit_solution(4807908578650684487)
XLA Ops:
  0.6 55.0 %relay.1 = (f32[512,512]{1,0:T(8,128)S(1)}, bf16[8,8192]{1,0:T(8,128)(2,1)S(1)}) custom-call(bf16[8,8192]{1,0:T(8,128)(2,1)} %bitcast.10, bf16[512,8192]{1,0:T(8,128)(2,1)} %bitcast.9, s32[2,8]{1,0:T(2,128)} %bitcast.11, s32[16]{0:T(128)} %owner_hbm.1), custom_call_target="tpu_custom_call" | custom-call | tf_op jit(solution)/shard_map/relay/pallas_call | solution.py:335
  55.6 1.0 %copy.8 = f32[1,1,512,512]{3,2,1,0:T(8,128)} copy(f32[1,1,512,512]{3,2,1,0:T(8,128)S(1)} %bitcast.7) | data formatting | bytes 2097152
  56.6 0.7 %copy.9 = bf16[1,8,8192]{2,1,0:T(8,128)(2,1)} copy(bf16[1,8,8192]{2,1,0:T(8,128)(2,1)S(1)} %bitcast.8) | data formatting | bytes 262144

commit v3 on v0

v3 whole, which is shorter than its diff:
```python
import functools

import jax
import jax.numpy as jnp
from jax import lax
from jax.experimental import pallas as pl
from jax.experimental.pallas import tpu as pltpu
from jax.sharding import PartitionSpec as P

D = 8192
BLK = 512
HALF = 256
NB = 8
STEPS = 2
TOKENS = 128
DP = 16
CHIPS = 8
TOK = TOKENS // DP
ROWS = 2 * TOK
BANDS = D // BLK
CORES = 2
ROWS0 = TOKENS // CORES
SIDE = BANDS // CORES
CHUNKS = 2
PER = SIDE // CHUNKS
MESH = pl.DeviceIdType.MESH
F32 = jnp.float32
BF16 = jnp.bfloat16

ROUTES = (
    ((1, 1), (0, 1), 5, ()),
    ((1, 3), (0, 3), 6, ()),
    ((1, 2), (1, 0), 4, ()),
    ((0, 1), (0, 1), 0, ()),
    ((0, 3), (0, 3), 1, ()),
    ((0, 2), (0, 2), 2, (4,)),
    ((1, 0), (1, 0), 3, (5, 6)),
    ((0, 0), None, None, ()),
)
SLOTS = 7
CHIP_ORDER = ((1, 2), (1, 1), (1, 3), (0, 2), (1, 0), (0, 1), (0, 3), (0, 0))
PEERS = tuple(r for r in range(DP) if r != DP - 2)
FINAL = 4
SENDER = tuple(next(k for k in range(SLOTS) if ROUTES[k][2] == slot) for slot in range(SLOTS))


def folded(rows):
    cut = rows.reshape(rows.shape[0] // TOK, TOK, BLK)
    return jnp.concatenate([cut[:, :, :HALF], cut[:, :, HALF:]], axis=1)


def unfolded(blocks):
    wide = blocks.astype(F32)
    flat = jnp.concatenate([wide[:, :TOK], wide[:, TOK:]], axis=2)
    return flat.reshape(blocks.shape[0] * TOK, BLK)


def kernel(
    g_hbm, w_hbm, band_hbm, owner_hbm, factors_ref, gout_ref,
    g_ref, band_ref, owner_ref, w, gtok, banded, x0, x1_out, x1,
    sib_out0, sib_in0, own0, rs_out0, rs_in0,
    sib_out1, sib_in1, own1, rs_out1, rs_in1,
    n0_out, right0, g1tok, own_out, own_in, fin, right1, gout_in,
    l0_out, rl_out, r1_out, l0_in, rl_in, r1_in,
    in_sem, w_sem, a2a_send, a2a_recv, sib_send0, sib_recv0, sib_send1, sib_recv1,
    rs_send0, rs_recv0, rs_send1, rs_recv1, fin_recv, pass_send, pass_recv, one_send, one_recv,
):
    sec = lax.axis_index("section")
    me = lax.axis_index("dp")
    secs = lax.axis_size("section")
    core = me % 2
    y = (me // 2) % 4
    x = me // 8
    before = (sec + secs - 1) % secs
    after = (sec + 1) % secs

    xs = (x, 1 - x)
    ys = tuple((y + d) % 4 for d in range(4))
    chips = {(dx, dy): xs[dx] * 4 + ys[dy] for dx in range(2) for dy in range(4)}

    def chip(dx, dy):
        return chips[dx, dy]

    here = chips[0, 0]
    sibling = here * 2 + 1 - core
    first = core == 0

    def peer(r):
        far = chips[CHIP_ORDER[r // 2]] * 2
        return far + (core if r % 2 == 0 else 1 - core)

    def remote(src, dst, send, recv, device):
        return pltpu.make_async_remote_copy(
            src_ref=src, dst_ref=dst, send_sem=send, recv_sem=recv,
            device_id=device, device_id_type=MESH,
        )

    def w_copy(k):
        cols = pl.ds(pl.multiple_of(chip(*ROUTES[k][0]) * 2 * BLK, 2 * BLK), 2 * BLK)
        return pltpu.make_async_copy(w_hbm.at[:, cols], w.at[:, cols], w_sem.at[k])

    barrier = pltpu.get_barrier_semaphore()
    for r in PEERS:
        pl.semaphore_signal(barrier, inc=1, device_id=(sec, peer(r)), device_id_type=MESH)
    for other_section in (before, after):
        pl.semaphore_signal(barrier, inc=1, device_id=(other_section, me), device_id_type=MESH)

    g_in = pltpu.make_async_copy(g_hbm, g_ref, in_sem.at[0])
    band_in = pltpu.make_async_copy(band_hbm, band_ref, in_sem.at[1])
    owner_in = pltpu.make_async_copy(owner_hbm, owner_ref, in_sem.at[2])
    g_in.start()
    band_in.start()
    owner_in.start()
    for k in range(CHIPS):
        w_copy(k).start()
    g_in.wait()
    wide = g_ref[...].astype(F32)
    for b in range(BANDS):
        gtok[b] = folded(wide[:, b * BLK:(b + 1) * BLK])[0].astype(BF16)

    pl.semaphore_wait(barrier, DP - 1 + 2)

    def all_of(ref, sem):
        pltpu.make_async_copy(ref, ref, sem).wait()

    def exchange(which, out, into):
        def start():
            for r in PEERS:
                q = peer(r)
                remote(out.at[q], into.at[me], a2a_send.at[which], a2a_recv.at[which], (sec, q)).start()
            into[me] = out[me]

        def recv():
            all_of(into.at[pl.ds(0, DP - 1)], a2a_recv.at[which])

        def sent():
            all_of(out.at[pl.ds(0, DP - 1)], a2a_send.at[which])

        return start, recv, sent

    a_start, a_recv, a_sent = exchange(0, gtok, banded)
    l0_start, l0_recv, l0_sent = exchange(2, l0_out, l0_in)
    rl_start, rl_recv, rl_sent = exchange(4, rl_out, rl_in)
    r1_start, r1_recv, r1_sent = exchange(5, r1_out, r1_in)

    a_start()
    band_in.wait()
    owner_in.wait()

    def select(out, source, column, part=None):
        for q in range(DP):
            slot = owner_ref[q]
            index = band_ref[column, slot % NB]
            if column == 1:
                index = index + (slot // NB) * BANDS
            if part is None:
                out[q] = source[index]
            else:
                out[q, part] = source[index]

    select(l0_out, gtok, 0)
    l0_start()
    a_recv()
    by_core = banded[...].reshape(CHIPS, CORES, ROWS, HALF)
    for h in range(CORES):
        x0[h] = unfolded(by_core[:, h]).astype(BF16)

    def to_sibling0(h, k):
        return remote(sib_out0.at[h, k], sib_in0.at[h, k], sib_send0, sib_recv0.at[h, k], (sec, sibling))

    def rs0(h, k):
        _, to, slot, _ = ROUTES[k]
        return remote(
            rs_out0.at[h, k], rs_in0.at[h, slot], rs_send0, rs_recv0.at[h, slot],
            (sec, chip(*to) * 2 + core),
        )

    def arrived0(h, slot):
        rs0(h, SENDER[slot]).wait_recv()
        return rs_in0[h, slot].astype(F32)

    def compute0(h, k):
        m = chip(*ROUTES[k][0])
        if h == 0:
            w_copy(k).wait()
        cols = pl.ds(pl.multiple_of(m * 2 * BLK, 2 * BLK), 2 * BLK)
        part = jnp.dot(x0[h], w[:, cols], preferred_element_type=F32)
        sib_out0[h, k] = jnp.where(first, part[:, BLK:], part[:, :BLK]).astype(BF16)
        to_sibling0(h, k).start()
        own0[h, k] = jnp.where(first, part[:, :BLK], part[:, BLK:])

    def finish0(h, k):
        to_sibling0(h, k).wait_recv()
        total = own0[h, k] + sib_in0[h, k].astype(F32)
        for slot in ROUTES[k][3]:
            total = total + arrived0(h, slot)
        rs_out0[h, k] = total.astype(BF16)
        rs0(h, k).start()

    def band_pass(h):
        return remote(x1_out.at[h], x1.at[h], pass_send.at[h], pass_recv.at[h], (before, me))

    def token_copy(h, c):
        to = chips[CHIP_ORDER[c]]
        return remote(
            n0_out.at[to, h], right0.at[BANDS + me], a2a_send.at[1], a2a_recv.at[1],
            (sec, to * 2 + h),
        )

    def last0(h):
        k = CHIPS - 1
        to_sibling0(h, k).wait_recv()
        total = own0[h, k] + sib_in0[h, k].astype(F32) + x0[h].astype(F32)
        for slot in range(FINAL):
            total = total + arrived0(h, slot)
        x1_out[h] = total.astype(BF16)
        band_pass(h).start()
        n0_out[:, h] = folded(total).astype(BF16)

    def spread(h):
        for c in range(CHIPS - 1):
            token_copy(h, c).start()

        @pl.when(core == h)
        def _():
            right0[BANDS + me] = n0_out[here, h]

        @pl.when(core != h)
        def _():
            token_copy(h, CHIPS - 1).start()

    token_pass = remote(right0.at[pl.ds(BANDS, BANDS)], g1tok, one_send.at[0], one_recv.at[0], (before, me))

    def tokens_on(h):
        @pl.when(core == h)
        def _():
            all_of(right0.at[pl.ds(BANDS, DP - 1)], a2a_recv.at[1])
            token_pass.start()

    def tokens_in(h):
        @pl.when(core == h)
        def _():
            token_pass.wait_recv()

    def to_sibling1(h, j):
        return remote(sib_out1.at[h, j], sib_in1.at[h, j], sib_send1, sib_recv1.at[h, j], (sec, sibling))

    def rs1(h, j, k):
        _, to, slot, _ = ROUTES[k]
        if slot < FINAL:
            return remote(rs_out1.at[h, j, k], fin.at[core, j, slot], rs_send1, fin_recv, (sec, chip(*to) * 2 + h))
        return remote(
            rs_out1.at[h, j, k], rs_in1.at[h, j, slot - FINAL], rs_send1, rs_recv1.at[h, j, slot - FINAL],
            (sec, chip(*to) * 2 + core),
        )

    def arrived1(h, j, slot):
        rs1(h, j, SENDER[slot]).wait_recv()
        return rs_in1[h, j, slot - FINAL].astype(F32)

    def to_owner(j):
        return remote(own_out.at[j], own_in.at[j], one_send.at[1], one_recv.at[1], (sec, sibling))

    def compute1(h, j):
        width = PER * BLK

        def part(c):
            cols = pl.ds(pl.multiple_of(c * SIDE * BLK + j * width, width), width)
            return jnp.dot(x1[h], w[:, cols], preferred_element_type=F32)

        other = part(1 - core)
        for e in range(PER):
            sib_out1[h, j, :, e] = folded(other[:, e * BLK:(e + 1) * BLK]).astype(BF16)
        to_sibling1(h, j).start()
        mine = part(core)
        for e in range(PER):
            own1[h, j, :, e] = folded(mine[:, e * BLK:(e + 1) * BLK])

    def finish1(h, j, ks):
        for k in ks:
            m = chip(*ROUTES[k][0])
            total = own1[h, j, m] + sib_in1[h, j, m].astype(F32)
            for slot in ROUTES[k][3]:
                total = total + arrived1(h, j, slot)
            rs_out1[h, j, k] = total.astype(BF16)
            rs1(h, j, k).start()

    def early1(h, j):
        to_sibling1(h, j).wait_recv()
        finish1(h, j, (0, 1, 2, 3, 4))

        @pl.when(core != h)
        def _():
            own_out[j] = (own1[h, j, here] + sib_in1[h, j, here].astype(F32)).astype(BF16)
            to_owner(j).start()

    def late1(h, j):
        finish1(h, j, (5, 6))

    gout_copy = remote(right1.at[pl.ds(BANDS, BANDS)], gout_in, one_send.at[2], one_recv.at[2], (before, me))

    def last1(h):
        @pl.when(core == h)
        def _():
            all_of(own_in, one_recv.at[1])
            all_of(fin, fin_recv)
            for p in range(CORES):
                for j in range(CHUNKS):
                    at = p * SIDE + j * PER
                    if p == h:
                        total = own1[h, j, here] + sib_in1[h, j, here].astype(F32)
                    else:
                        total = own_in[j].astype(F32)
                    total = total + g1tok[at:at + PER].astype(F32)
                    for slot in range(FINAL):
                        total = total + fin[p, j, slot].astype(F32)
                    right1[BANDS + at:BANDS + at + PER] = total.astype(BF16)
            gout_copy.start()
            select(r1_out, right1, 1)
            r1_start()

    compute0(0, 0)
    compute0(0, 1)
    compute0(0, 2)
    finish0(0, 0)
    compute0(0, 3)
    finish0(0, 1)
    compute0(0, 4)
    finish0(0, 2)
    compute0(0, 5)
    finish0(0, 3)
    compute0(0, 6)
    finish0(0, 4)
    compute0(0, 7)
    compute0(1, 0)
    finish0(0, 5)
    compute0(1, 1)
    finish0(0, 6)
    compute0(1, 2)
    finish0(1, 0)
    compute0(1, 3)
    finish0(1, 1)
    compute0(1, 4)
    finish0(1, 2)
    compute0(1, 5)
    finish0(1, 3)
    compute0(1, 6)
    finish0(1, 4)
    compute0(1, 7)
    last0(0)
    finish0(1, 5)
    finish0(1, 6)
    spread(0)
    right0[:BANDS] = gtok[...]
    band_pass(0).wait_recv()
    compute1(0, 0)
    compute1(0, 1)
    early1(0, 0)
    last0(1)
    spread(1)
    early1(0, 1)
    late1(0, 0)
    tokens_on(0)
    late1(0, 1)
    band_pass(1).wait_recv()
    compute1(1, 0)
    compute1(1, 1)
    early1(1, 0)
    early1(1, 1)
    tokens_on(1)
    late1(1, 0)
    late1(1, 1)
    tokens_in(0)
    tokens_in(1)
    right1[:BANDS] = g1tok[...]
    last1(0)
    select(rl_out, right0, 1, 0)
    select(rl_out, g1tok, 0, 1)
    rl_start()
    last1(1)

    def gram(left, right):
        return lax.dot_general(
            unfolded(left).astype(BF16), unfolded(right).astype(BF16),
            (((0,), (0,)), ((), ())), preferred_element_type=F32,
        )

    l0_recv()
    rl_recv()
    factors_ref[...] = gram(l0_in[...], rl_in[:, 0])
    gout_copy.wait_recv()
    for b in range(BANDS):
        gout_ref[:, b * BLK:(b + 1) * BLK] = unfolded(gout_in[b:b + 1]).astype(BF16)
    r1_recv()
    factors_ref[...] = (factors_ref[...] + gram(rl_in[:, 1], r1_in[...])) * (1.0 / (TOKENS * STEPS))

    a_sent()
    l0_sent()
    rl_sent()
    r1_sent()
    token_pass.wait_send()
    gout_copy.wait_send()
    all_of(own_out, one_send.at[1])
    all_of(n0_out.at[:CHIPS - 1], a2a_send.at[1])
    all_of(n0_out.at[0, 0], a2a_send.at[1])
    for h in range(CORES):
        band_pass(h).wait_send()
    all_of(sib_out0, sib_send0)
    all_of(rs_out0, rs_send0)
    all_of(sib_out1, sib_send1)
    all_of(rs_out1, rs_send1)


def shards(grad_in, weights, band_index, owner):
    vmem = pl.BlockSpec(memory_space=pltpu.VMEM)
    tok = (BANDS, ROWS, HALF)
    dma = pltpu.SemaphoreType.DMA
    factors, gout = pl.pallas_call(
        kernel,
        out_shape=(
            pltpu.VMEM((BLK, BLK), F32),
            pltpu.VMEM((TOK, D), BF16),
        ),
        in_specs=[pl.BlockSpec(memory_space=pl.ANY)] * 4,
        out_specs=(vmem, vmem),
        scratch_shapes=[
            pltpu.VMEM((TOK, D), BF16),
            pltpu.SMEM((2, NB), jnp.int32),
            pltpu.SMEM((DP,), jnp.int32),
            pltpu.VMEM((BLK, D), BF16),
            pltpu.VMEM(tok, BF16),
            pltpu.VMEM(tok, BF16),
            pltpu.VMEM((CORES, ROWS0, BLK), BF16),
            pltpu.VMEM((CORES, ROWS0, BLK), BF16),
            pltpu.VMEM((CORES, ROWS0, BLK), BF16),
            pltpu.VMEM((CORES, CHIPS, ROWS0, BLK), BF16),
            pltpu.VMEM((CORES, CHIPS, ROWS0, BLK), BF16),
            pltpu.VMEM((CORES, CHIPS, ROWS0, BLK), F32),
            pltpu.VMEM((CORES, SLOTS, ROWS0, BLK), BF16),
            pltpu.VMEM((CORES, SLOTS, ROWS0, BLK), BF16),
            pltpu.VMEM((CORES, CHUNKS, CHIPS, PER, ROWS, HALF), BF16),
            pltpu.VMEM((CORES, CHUNKS, CHIPS, PER, ROWS, HALF), BF16),
            pltpu.VMEM((CORES, CHUNKS, CHIPS, PER, ROWS, HALF), F32),
            pltpu.VMEM((CORES, CHUNKS, SLOTS, PER, ROWS, HALF), BF16),
            pltpu.VMEM((CORES, CHUNKS, SLOTS - FINAL, PER, ROWS, HALF), BF16),
            pltpu.VMEM((CHIPS, CORES, ROWS, HALF), BF16),
            pltpu.VMEM((2 * BANDS, ROWS, HALF), BF16),
            pltpu.VMEM(tok, BF16),
            pltpu.VMEM((CHUNKS, PER, ROWS, HALF), BF16),
            pltpu.VMEM((CHUNKS, PER, ROWS, HALF), BF16),
            pltpu.VMEM((CORES, CHUNKS, FINAL, PER, ROWS, HALF), BF16),
            pltpu.VMEM((2 * BANDS, ROWS, HALF), BF16),
            pltpu.VMEM(tok, BF16),
            pltpu.VMEM(tok, BF16),
            pltpu.VMEM((DP, 2, ROWS, HALF), BF16),
            pltpu.VMEM(tok, BF16),
            pltpu.VMEM(tok, BF16),
            pltpu.VMEM((DP, 2, ROWS, HALF), BF16),
            pltpu.VMEM(tok, BF16),
            dma((3,)),
            dma((CHIPS,)),
            dma((6,)),
            dma((6,)),
            dma,
            dma((CORES, CHIPS)),
            dma,
            dma((CORES, CHUNKS)),
            dma,
            dma((CORES, SLOTS)),
            dma,
            dma((CORES, CHUNKS, SLOTS - FINAL)),
            dma,
            dma((CORES,)),
            dma((CORES,)),
            dma((3,)),
            dma((3,)),
        ],
        compiler_params=pltpu.CompilerParams(
            collective_id=0, has_side_effects=True, vmem_limit_bytes=58 * 2 ** 20,
        ),
        name="relay",
    )(grad_in[0], weights[0], band_index[0].T, owner)
    return factors[None, None], gout[None]


def solution(mesh):
    return jax.shard_map(
        shards,
        mesh=mesh,
        in_specs=(
            P("section", "dp", None),
            P("section", "dp", None),
            P("section", None, None),
            P(),
        ),
        out_specs=(P("section", "dp", None, None), P("section", "dp", None)),
        check_vma=False,
    )
```

time: 338 us -> 51.9 us (0.15)
  waiting for transfers between devices: 210 us -> 0 us
  Pallas kernels: 0 us -> 49.2 us
  matrix products: 29.7 us -> 0 us
  other arithmetic: 26.8 us -> 0 us
  blocking collectives: 26.7 us -> 0 us
  local copies, waits for them, and re-layouts: 19.6 us -> 1.63 us
  between operations: 13.9 us -> 0.64 us
  starting transfers between devices: 10.6 us -> 0 us
    reduce_scatter x3 -> x0, waiting for transfers between devices: 206 us -> none  [the longest x2 112 us: shards(): lax.psum_scatter(jnp.dot(banded, w_rows, preferred_element_type=jnp.float...]
    pallas_call x0 -> x1, Pallas kernels: none -> 49.2 us  [shards(): pl.pallas_call(kernel, out_shape=(pltpu.VMEM((BLK, BLK), F32), pltpu.VMEM...]
    dot_general x6 -> x0, matrix products: 29.7 us -> none  [the longest x2 13.5 us: shards(): jnp.dot(banded, w_rows, preferred_element_type=jnp.float32)]
    all_to_all x2 -> x0, blocking collectives: 26.7 us -> none  [shards(): banded = lax.all_to_all(held, 'dp', split_axis=1, concat_axis=0, tiled=True)]
    gather x7 -> x0, local copies, waits for them, and re-layouts: 17.1 us -> none  [the longest x1 13.8 us: shards(): ordered = jnp.take(totals, owner, axis=0) / float(all_tokens * STEPS)]
    add x1 -> x0, other arithmetic: 12.7 us -> none  [shards(): totals = totals + gram_blocks(held, fresh, pairs)]
    div x1 -> x0, other arithmetic: 12.1 us -> none  [shards(): ordered = jnp.take(totals, owner, axis=0) / float(all_tokens * STEPS)]
    ppermute x2 -> x0, starting transfers between devices: 10.3 us -> none  [passed_along(): return lax.ppermute(value, axis, pairs)]
  transfers between devices with their start and end apart: 5 -> 0, of which waited for: 5 -> 0; matrix products, arithmetic and copies ran while one was open for 5% -> 0% of each run, Pallas kernels for 0% -> 0%
where the time goes in v3:
time: 51.9 us; the launch traced here: 51.5 us
  Pallas kernels  49.2 us (95%)
  local copies, waits for them, and re-layouts  1.63 us (3%)
  between operations  0.64 us (1%)
    pallas_call x1, Pallas kernels, shards(): pl.pallas_call(kernel, out_shape=(pltpu.VMEM((BLK, BLK), F32), pltpu.VMEM...  49.2 us
    unnamed x2, local copies, waits for them, and re-layouts  1.63 us

profile of v3, /device:TPU:1, one launch (start us, length us, event | category | flops | bytes accessed | tf_op | source)
XLA Modules:
  0.0 51.5 jit_solution(16901136236018050334)
XLA Ops:
  0.6 49.2 %relay.1 = (f32[512,512]{1,0:T(8,128)S(1)}, bf16[8,8192]{1,0:T(8,128)(2,1)S(1)}) custom-call(bf16[8,8192]{1,0:T(8,128)(2,1)} %bitcast.10, bf16[512,8192]{1,0:T(8,128)(2,1)} %bitcast.9, s32[2,8]{1,0:T(2,128)} %bitcast.11, s32[16]{0:T(128)} %owner_hbm.1), custom_call_target="tpu_custom_call" | custom-call | tf_op jit(solution)/shard_map/relay/pallas_call | solution.py:418
  49.8 1.0 %copy.8 = f32[1,1,512,512]{3,2,1,0:T(8,128)} copy(f32[1,1,512,512]{3,2,1,0:T(8,128)S(1)} %bitcast.7) | data formatting | bytes 2097152
  50.8 0.7 %copy.9 = bf16[1,8,8192]{2,1,0:T(8,128)(2,1)} copy(bf16[1,8,8192]{2,1,0:T(8,128)(2,1)S(1)} %bitcast.8) | data formatting | bytes 262144

commit v4 on v3

--- a/solution.py
+++ b/solution.py
@@ -21,16 +21,16 @@
 CORES = 2
 ROWS0 = TOKENS // CORES
 SIDE = BANDS // CORES
-CHUNKS = 2
+CHUNKS = 1
 PER = SIDE // CHUNKS
 MESH = pl.DeviceIdType.MESH
 F32 = jnp.float32
 BF16 = jnp.bfloat16
 
 ROUTES = (
+    ((1, 2), (1, 0), 4, ()),
     ((1, 1), (0, 1), 5, ()),
     ((1, 3), (0, 3), 6, ()),
-    ((1, 2), (1, 0), 4, ()),
     ((0, 1), (0, 1), 0, ()),
     ((0, 3), (0, 3), 1, ()),
     ((0, 2), (0, 2), 2, (4,)),
@@ -165,8 +165,18 @@
     for h in range(CORES):
         x0[h] = unfolded(by_core[:, h]).astype(BF16)
 
-    def to_sibling0(h, k):
-        return remote(sib_out0.at[h, k], sib_in0.at[h, k], sib_send0, sib_recv0.at[h, k], (sec, sibling))
+    def to_sibling0(h, n):
+        pair = pl.ds(2 * n, 2)
+        return remote(
+            sib_out0.at[h, pair], sib_in0.at[h, pair], sib_send0, sib_recv0.at[h, n], (sec, sibling),
+        )
+
+    shared = set()
+
+    def shared0(h, k):
+        if (h, k // 2) not in shared:
+            shared.add((h, k // 2))
+            to_sibling0(h, k // 2).wait_recv()
 
     def rs0(h, k):
         _, to, slot, _ = ROUTES[k]
@@ -179,23 +189,29 @@
         rs0(h, SENDER[slot]).wait_recv()
         return rs_in0[h, slot].astype(F32)
 
-    def compute0(h, k):
-        m = chip(*ROUTES[k][0])
-        if h == 0:
-            w_copy(k).wait()
-        cols = pl.ds(pl.multiple_of(m * 2 * BLK, 2 * BLK), 2 * BLK)
-        part = jnp.dot(x0[h], w[:, cols], preferred_element_type=F32)
-        sib_out0[h, k] = jnp.where(first, part[:, BLK:], part[:, :BLK]).astype(BF16)
-        to_sibling0(h, k).start()
-        own0[h, k] = jnp.where(first, part[:, :BLK], part[:, BLK:])
-
-    def finish0(h, k):
-        to_sibling0(h, k).wait_recv()
-        total = own0[h, k] + sib_in0[h, k].astype(F32)
-        for slot in ROUTES[k][3]:
-            total = total + arrived0(h, slot)
-        rs_out0[h, k] = total.astype(BF16)
-        rs0(h, k).start()
+    def compute0(h, n):
+        for k in (2 * n, 2 * n + 1):
+            if h == 0:
+                w_copy(k).wait()
+        for k in (2 * n, 2 * n + 1):
+            cols = pl.ds(pl.multiple_of(chip(*ROUTES[k][0]) * 2 * BLK, 2 * BLK), 2 * BLK)
+            part = jnp.dot(x0[h], w[:, cols], preferred_element_type=F32)
+            sib_out0[h, k] = jnp.where(first, part[:, BLK:], part[:, :BLK]).astype(BF16)
+            own0[h, k] = jnp.where(first, part[:, :BLK], part[:, BLK:])
+        to_sibling0(h, n).start()
+
+    def finish0(h, *ks):
+        for k in ks:
+            shared0(h, k)
+            for slot in ROUTES[k][3]:
+                rs0(h, SENDER[slot]).wait_recv()
+        for k in ks:
+            total = own0[h, k] + sib_in0[h, k].astype(F32)
+            for slot in ROUTES[k][3]:
+                total = total + rs_in0[h, slot].astype(F32)
+            rs_out0[h, k] = total.astype(BF16)
+        for k in ks:
+            rs0(h, k).start()
 
     def band_pass(h):
         return remote(x1_out.at[h], x1.at[h], pass_send.at[h], pass_recv.at[h], (before, me))
@@ -209,7 +225,7 @@
 
     def last0(h):
         k = CHIPS - 1
-        to_sibling0(h, k).wait_recv()
+        shared0(h, k)
         total = own0[h, k] + sib_in0[h, k].astype(F32) + x0[h].astype(F32)
         for slot in range(FINAL):
             total = total + arrived0(h, slot)
@@ -321,32 +337,20 @@
 
     compute0(0, 0)
     compute0(0, 1)
+    finish0(0, 0, 1)
     compute0(0, 2)
-    finish0(0, 0)
+    finish0(0, 2, 3)
     compute0(0, 3)
-    finish0(0, 1)
-    compute0(0, 4)
-    finish0(0, 2)
-    compute0(0, 5)
-    finish0(0, 3)
-    compute0(0, 6)
     finish0(0, 4)
-    compute0(0, 7)
     compute0(1, 0)
     finish0(0, 5)
+    finish0(0, 6)
     compute0(1, 1)
-    finish0(0, 6)
+    finish0(1, 0, 1)
     compute0(1, 2)
-    finish0(1, 0)
+    finish0(1, 2, 3)
     compute0(1, 3)
-    finish0(1, 1)
-    compute0(1, 4)
-    finish0(1, 2)
-    compute0(1, 5)
-    finish0(1, 3)
-    compute0(1, 6)
     finish0(1, 4)
-    compute0(1, 7)
     last0(0)
     finish0(1, 5)
     finish0(1, 6)
@@ -354,22 +358,16 @@
     right0[:BANDS] = gtok[...]
     band_pass(0).wait_recv()
     compute1(0, 0)
-    compute1(0, 1)
     early1(0, 0)
     last0(1)
     spread(1)
-    early1(0, 1)
     late1(0, 0)
     tokens_on(0)
-    late1(0, 1)
     band_pass(1).wait_recv()
     compute1(1, 0)
-    compute1(1, 1)
     early1(1, 0)
-    early1(1, 1)
     tokens_on(1)
     late1(1, 0)
-    late1(1, 1)
     tokens_in(0)
     tokens_in(1)
     right1[:BANDS] = g1tok[...]
@@ -391,13 +389,9 @@
     gout_copy.wait_recv()
     for b in range(BANDS):
         gout_ref[:, b * BLK:(b + 1) * BLK] = unfolded(gout_in[b:b + 1]).astype(BF16)
-    r1_recv()
-    factors_ref[...] = (factors_ref[...] + gram(rl_in[:, 1], r1_in[...])) * (1.0 / (TOKENS * STEPS))
-
     a_sent()
     l0_sent()
     rl_sent()
-    r1_sent()
     token_pass.wait_send()
     gout_copy.wait_send()
     all_of(own_out, one_send.at[1])
@@ -409,6 +403,10 @@
     all_of(rs_out0, rs_send0)
     all_of(sib_out1, sib_send1)
     all_of(rs_out1, rs_send1)
+    r1_recv()
+    factors_ref[...] = (factors_ref[...] + gram(rl_in[:, 1], r1_in[...])) * (1.0 / (TOKENS * STEPS))
+
+    r1_sent()
 
 
 def shards(grad_in, weights, band_index, owner):
@@ -462,7 +460,7 @@
             dma((6,)),
             dma((6,)),
             dma,
-            dma((CORES, CHIPS)),
+            dma((CORES, CHIPS // 2)),
             dma,
             dma((CORES, CHUNKS)),
             dma,

time: 51.9 us -> 51 us (0.983)
  no operation moved by 1% of the time
where the time goes in v4:
time: 51 us
  Pallas kernels  48.7 us (95%)
  local copies, waits for them, and re-layouts  1.63 us (3%)
  between operations  0.64 us (1%)
    pallas_call x1, Pallas kernels, shards(): pl.pallas_call(kernel, out_shape=(pltpu.VMEM((BLK, BLK), F32), pltpu.VMEM...  48.7 us
    unnamed x2, local copies, waits for them, and re-layouts  1.63 us

profile of v4, /device:TPU:1, one launch (start us, length us, event | category | flops | bytes accessed | tf_op | source)
XLA Modules:
  0.0 51.0 jit_solution(13170608473410737875)
XLA Ops:
  0.6 48.7 %relay.1 = (f32[512,512]{1,0:T(8,128)S(1)}, bf16[8,8192]{1,0:T(8,128)(2,1)S(1)}) custom-call(bf16[8,8192]{1,0:T(8,128)(2,1)} %bitcast.10, bf16[512,8192]{1,0:T(8,128)(2,1)} %bitcast.9, s32[2,8]{1,0:T(2,128)} %bitcast.11, s32[16]{0:T(128)} %owner_hbm.1), custom_call_target="tpu_custom_call" | custom-call | tf_op jit(solution)/shard_map/relay/pallas_call | solution.py:416
  49.3 1.0 %copy.8 = f32[1,1,512,512]{3,2,1,0:T(8,128)} copy(f32[1,1,512,512]{3,2,1,0:T(8,128)S(1)} %bitcast.7) | data formatting | bytes 2097152
  50.3 0.7 %copy.9 = bf16[1,8,8192]{2,1,0:T(8,128)(2,1)} copy(bf16[1,8,8192]{2,1,0:T(8,128)(2,1)S(1)} %bitcast.8) | data formatting | bytes 262144

commit v5 on v4

--- a/solution.py
+++ b/solution.py
@@ -61,7 +61,7 @@
     sib_out0, sib_in0, own0, rs_out0, rs_in0,
     sib_out1, sib_in1, own1, rs_out1, rs_in1,
     n0_out, right0, g1tok, own_out, own_in, fin, right1, gout_in,
-    l0_out, rl_out, r1_out, l0_in, rl_in, r1_in,
+    l0_out, r0_out, l1_out, r1_out, l0_in, r0_in, l1_in, r1_in,
     in_sem, w_sem, a2a_send, a2a_recv, sib_send0, sib_recv0, sib_send1, sib_recv1,
     rs_send0, rs_recv0, rs_send1, rs_recv1, fin_recv, pass_send, pass_recv, one_send, one_recv,
 ):
@@ -140,23 +140,21 @@
 
     a_start, a_recv, a_sent = exchange(0, gtok, banded)
     l0_start, l0_recv, l0_sent = exchange(2, l0_out, l0_in)
-    rl_start, rl_recv, rl_sent = exchange(4, rl_out, rl_in)
+    r0_start, r0_recv, r0_sent = exchange(3, r0_out, r0_in)
+    l1_start, l1_recv, l1_sent = exchange(4, l1_out, l1_in)
     r1_start, r1_recv, r1_sent = exchange(5, r1_out, r1_in)
 
     a_start()
     band_in.wait()
     owner_in.wait()
 
-    def select(out, source, column, part=None):
+    def select(out, source, column):
         for q in range(DP):
             slot = owner_ref[q]
             index = band_ref[column, slot % NB]
             if column == 1:
                 index = index + (slot // NB) * BANDS
-            if part is None:
-                out[q] = source[index]
-            else:
-                out[q, part] = source[index]
+            out[q] = source[index]
 
     select(l0_out, gtok, 0)
     l0_start()
@@ -252,6 +250,9 @@
         def _():
             all_of(right0.at[pl.ds(BANDS, DP - 1)], a2a_recv.at[1])
             token_pass.start()
+            if h == 0:
+                select(r0_out, right0, 1)
+                r0_start()
 
     def tokens_in(h):
         @pl.when(core == h)
@@ -372,9 +373,14 @@
     tokens_in(1)
     right1[:BANDS] = g1tok[...]
     last1(0)
-    select(rl_out, right0, 1, 0)
-    select(rl_out, g1tok, 0, 1)
-    rl_start()
+
+    @pl.when(core == 1)
+    def _():
+        select(r0_out, right0, 1)
+        r0_start()
+
+    select(l1_out, g1tok, 0)
+    l1_start()
     last1(1)
 
     def gram(left, right):
@@ -384,14 +390,16 @@
         )
 
     l0_recv()
-    rl_recv()
-    factors_ref[...] = gram(l0_in[...], rl_in[:, 0])
+    r0_recv()
+    l1_recv()
+    factors_ref[...] = gram(l0_in[...], r0_in[...])
     gout_copy.wait_recv()
     for b in range(BANDS):
         gout_ref[:, b * BLK:(b + 1) * BLK] = unfolded(gout_in[b:b + 1]).astype(BF16)
     a_sent()
     l0_sent()
-    rl_sent()
+    r0_sent()
+    l1_sent()
     token_pass.wait_send()
     gout_copy.wait_send()
     all_of(own_out, one_send.at[1])
@@ -404,7 +412,7 @@
     all_of(sib_out1, sib_send1)
     all_of(rs_out1, rs_send1)
     r1_recv()
-    factors_ref[...] = (factors_ref[...] + gram(rl_in[:, 1], r1_in[...])) * (1.0 / (TOKENS * STEPS))
+    factors_ref[...] = (factors_ref[...] + gram(l1_in[...], r1_in[...])) * (1.0 / (TOKENS * STEPS))
 
     r1_sent()
 
@@ -450,10 +458,12 @@
             pltpu.VMEM((2 * BANDS, ROWS, HALF), BF16),
             pltpu.VMEM(tok, BF16),
             pltpu.VMEM(tok, BF16),
-            pltpu.VMEM((DP, 2, ROWS, HALF), BF16),
-            pltpu.VMEM(tok, BF16),
-            pltpu.VMEM(tok, BF16),
-            pltpu.VMEM((DP, 2, ROWS, HALF), BF16),
+            pltpu.VMEM(tok, BF16),
+            pltpu.VMEM(tok, BF16),
+            pltpu.VMEM(tok, BF16),
+            pltpu.VMEM(tok, BF16),
+            pltpu.VMEM(tok, BF16),
+            pltpu.VMEM(tok, BF16),
             pltpu.VMEM(tok, BF16),
             dma((3,)),
             dma((CHIPS,)),

time: 51 us -> 50.8 us (level)
  no operation moved by 1% of the time
where the time goes in v5:
time: 50.8 us; the launch traced here: 50.7 us
  Pallas kernels  48.5 us (95%)
  local copies, waits for them, and re-layouts  1.63 us (3%)
  between operations  0.64 us (1%)
    pallas_call x1, Pallas kernels, shards(): pl.pallas_call(kernel, out_shape=(pltpu.VMEM((BLK, BLK), F32), pltpu.VMEM...  48.5 us
    unnamed x2, local copies, waits for them, and re-layouts  1.63 us

profile of v5, /device:TPU:1, one launch (start us, length us, event | category | flops | bytes accessed | tf_op | source)
XLA Modules:
  0.0 50.7 jit_solution(5804447862598840031)
XLA Ops:
  0.6 48.5 %relay.1 = (f32[512,512]{1,0:T(8,128)S(1)}, bf16[8,8192]{1,0:T(8,128)(2,1)S(1)}) custom-call(bf16[8,8192]{1,0:T(8,128)(2,1)} %bitcast.10, bf16[512,8192]{1,0:T(8,128)(2,1)} %bitcast.9, s32[2,8]{1,0:T(2,128)} %bitcast.11, s32[16]{0:T(128)} %owner_hbm.1), custom_call_target="tpu_custom_call" | custom-call | tf_op jit(solution)/shard_map/relay/pallas_call | solution.py:424
  49.1 1.0 %copy.8 = f32[1,1,512,512]{3,2,1,0:T(8,128)} copy(f32[1,1,512,512]{3,2,1,0:T(8,128)S(1)} %bitcast.7) | data formatting | bytes 2097152
  50.1 0.7 %copy.9 = bf16[1,8,8192]{2,1,0:T(8,128)(2,1)} copy(bf16[1,8,8192]{2,1,0:T(8,128)(2,1)S(1)} %bitcast.8) | data formatting | bytes 262144
